TPU v7x, 32 devices: a whole 2x2x4 slice. The times are simulated.
32 devices in a mesh: row: 8 (over y, x, core), col: 4 (over z).
Axes of the slice: x: 2, y: 2, z: 4, core: 2. Of those that a mesh axis runs over, the one named last changes fastest.
Arguments:
- trailing_in: float32 [2, 8, 256, 4, 4, 256], P(None, 'row', None, None, 'col'), may hold values from 0 to 4, as said below
Outputs:
- factored: float32 [2, 8, 256, 4, 4, 256], P(None, 'row', None, None, 'col')
Inputs may be any that keep to these rules, and one draw needn't show every extreme that they name: `trailing_in`: the matrix is symmetric and positive definite.
All inputs are finite; a program needn't handle non-finite values.
Results may differ from a plain program's by a relative error of at most 0.0003.
Values sent between devices are 32-bit elements; how exact they have to be, the bound alone decides.
No kernel may reach another device: no remote copies, remote signals or barrier semaphores. Data moves between devices by JAX's collectives and lax.ppermute only.
A program may use at most 64 MiB of HBM per device.

v0:
```python
import jax
import jax.numpy as jnp
from jax import lax
from jax.sharding import PartitionSpec as P

NB = 256


HIGHEST_PRECISION = lax.Precision.HIGHEST


def from_root(shard, axis, root):
    mine = lax.axis_index(axis) == root
    return lax.psum(jnp.where(mine, shard, jnp.zeros_like(shard)), axis)


def crossing_tiles(panel_rows, row_index, col_index):
    n_row = lax.axis_size("row")
    n_col = lax.axis_size("col")
    groups = n_row // n_col
    slot_index = row_index // n_col
    holder = row_index % n_col == col_index
    chosen = (jnp.arange(groups, dtype=jnp.int32) == slot_index) & holder
    buffer = jnp.where(chosen[None, :, None, None], panel_rows[:, None, :, :], jnp.float32(0.0))
    gathered = lax.psum(buffer, "row")
    return gathered.reshape(panel_rows.shape[0] * groups, NB, NB)


def panel_step(blocks, panel_index, tile_row, tile_col, row_index, col_index):
    n_row = lax.axis_size("row")
    n_col = lax.axis_size("col")
    root_row = panel_index % n_row
    root_col = panel_index % n_col
    local_row = panel_index // n_row
    local_col = panel_index // n_col
    corner = from_root(blocks[local_row, :, local_col, :], "row", root_row)
    factor_diag = jnp.linalg.cholesky(corner)
    column = blocks[:, :, local_col, :]
    flat = column.reshape(column.shape[0] * NB, NB)
    solved = jax.scipy.linalg.solve_triangular(factor_diag, flat.T, lower=True).T.reshape(
        column.shape
    )
    solved = jnp.where(
        (tile_row == panel_index)[:, None, None],
        factor_diag[None],
        jnp.where((tile_row < panel_index)[:, None, None], jnp.float32(0.0), solved),
    )
    panel_rows = from_root(solved, "col", root_col)
    panel_cols = crossing_tiles(panel_rows, row_index, col_index)
    owner = tile_col[local_col] == panel_index
    blocks = blocks.at[:, :, local_col, :].set(jnp.where(owner, solved, column))
    return (blocks, panel_rows, panel_cols)


def trailing(blocks, panel_rows, panel_cols, keep):
    products = jnp.einsum(
        "nho,tuo->nhtu",
        panel_rows,
        panel_cols,
        precision=HIGHEST_PRECISION,
        preferred_element_type=jnp.float32,
    )
    return blocks - jnp.where(keep[None, None, :, None], products, jnp.float32(0.0))


def on_device(trailing_in):
    n_row = lax.axis_size("row")
    n_col = lax.axis_size("col")
    row_index = lax.axis_index("row")
    col_index = lax.axis_index("col")
    loc_rows = trailing_in.shape[0]
    loc_cols = trailing_in.shape[3]
    blocks = trailing_in.reshape(loc_rows, NB, loc_cols, NB)
    tile_row = jnp.arange(loc_rows, dtype=jnp.int32) * n_row + row_index
    tile_col = jnp.arange(loc_cols, dtype=jnp.int32) * n_col + col_index
    keep_zero = tile_col > 0
    keep_one = tile_col > 1
    blocks, rows_zero, cols_zero = panel_step(blocks, 0, tile_row, tile_col, row_index, col_index)
    blocks = trailing(blocks, rows_zero, cols_zero, keep_zero)
    blocks, rows_one, cols_one = panel_step(blocks, 1, tile_row, tile_col, row_index, col_index)
    blocks = trailing(blocks, rows_one, cols_one, keep_one)
    lower_tiles = tile_row[:, None] >= tile_col[None, :]
    blocks = jnp.where(lower_tiles[:, None, :, None], blocks, jnp.float32(0.0))
    return blocks.reshape(loc_rows, 1, NB, loc_cols, 1, NB)


def solution(mesh):
    return jax.shard_map(
        on_device,
        mesh=mesh,
        in_specs=(P(None, "row", None, None, "col", None),),
        out_specs=P(None, "row", None, None, "col", None),
        check_vma=False,
    )
```

profile of v0, /device:TPU:0, one launch (start us, length us, event | category | flops | bytes accessed | tf_op | source)
XLA Modules:
  0.0 468.4 jit_solution(6390771194530619960)
XLA Ops:
  6.5 4.6 copy.12
  12.2 56.0 %all-reduce.8.cloned.1.call-done = f32[256,256]{0,1:T(8,128)} async-done(((f32[256,256]{0,1:T(8,128)}), f32[256,256]{0,1:T(8,128)}) %all-reduce.8.cloned.1.call-update) | async-done | bytes 262160 | tf_op jit(solution)/shard_map/psum | solution.py:14
  68.2 1.1 copy.13
  70.3 11.7 %cholesky.130 = f32[128,128]{1,0:T(8,128)S(1)} custom-call(f32[128,128]{1,0:T(8,128)S(1)} %cholesky.194), custom_call_target="Cholesky" | custom-call | tf_op jit(solution)/shard_map/jit(cholesky)/cholesky | solution.py:37
  82.1 9.8 %custom-call.13 = f32[1,128,128]{1,2,0:T(8,128)S(1)} custom-call(f32[1,128,128]{2,1,0:T(8,128)S(1)} %get-tuple-element.78), custom_call_target="InvertDiagBlocksLowerTriangular" | custom-call | tf_op jit(solution)/shard_map/jit(cholesky)/cholesky | solution.py:37
  92.4 11.7 %cholesky.147 = f32[128,128]{1,0:T(8,128)S(1)} custom-call(f32[128,128]{1,0:T(8,128)S(1)} %convolution_subtract_fusion.3), custom_call_target="Cholesky" | custom-call | tf_op jit(solution)/shard_map/jit(cholesky)/cholesky | solution.py:37
  106.3 4.3 while.6
  107.1 1.4 bitcast_dynamic-update-slice_fusion.4
  109.2 1.4 bitcast_dynamic-update-slice_fusion.4
  110.6 19.7 %custom-call.14 = f32[2,128,128]{1,2,0:T(8,128)S(1)} custom-call(f32[2,128,128]{2,1,0:T(8,128)S(1)} %get-tuple-element.45), custom_call_target="InvertDiagBlocksLowerTriangular" | custom-call | tf_op jit(solution)/shard_map/jit(_solve_triangular)/triangular_solve | solution.py:40
  133.0 37.7 %all-reduce.10.cloned.1.call-done = f32[2,256,256]{2,1,0:T(8,128)} async-done(((f32[2,256,256]{2,1,0:T(8,128)}), f32[2,256,256]{2,1,0:T(8,128)}) %all-reduce.10.cloned.1.call-update) | async-done | bytes 524304 | tf_op jit(solution)/shard_map/psum | solution.py:14
  170.8 2.2 broadcast_select_fusion.1
  175.0 1.3 select_dynamic-update-slice_fusion.1
  176.3 1.3 copy-done
  177.6 53.3 %all-reduce.12.cloned.1.call-done = f32[4,256,256]{2,1,0:T(8,128)} async-done(((f32[4,256,256]{2,1,0:T(8,128)}), f32[4,256,256]{2,1,0:T(8,128)}) %all-reduce.12.cloned.1.call-update) | async-done | bytes 1048592 | tf_op jit(solution)/shard_map/psum | solution.py:25
  230.9 3.8 select_subtract_fusion
  236.0 52.2 %all-reduce.14.cloned.1.call-done = f32[256,256]{0,1:T(8,128)} async-done(((f32[256,256]{0,1:T(8,128)}), f32[256,256]{0,1:T(8,128)}) %all-reduce.14.cloned.1.call-update) | async-done | bytes 262160 | tf_op jit(solution)/shard_map/psum | solution.py:14
  288.2 1.1 copy.20
  290.3 11.7 %cholesky.164 = f32[128,128]{1,0:T(8,128)S(1)} custom-call(f32[128,128]{1,0:T(8,128)S(1)} %cholesky.197), custom_call_target="Cholesky" | custom-call | tf_op jit(solution)/shard_map/jit(cholesky)/cholesky | solution.py:37
  302.1 9.8 %custom-call.15 = f32[1,128,128]{1,2,0:T(8,128)S(1)} custom-call(f32[1,128,128]{2,1,0:T(8,128)S(1)} %get-tuple-element.74), custom_call_target="InvertDiagBlocksLowerTriangular" | custom-call | tf_op jit(solution)/shard_map/jit(cholesky)/cholesky | solution.py:37
  312.4 11.7 %cholesky.181 = f32[128,128]{1,0:T(8,128)S(1)} custom-call(f32[128,128]{1,0:T(8,128)S(1)} %convolution_subtract_fusion.2), custom_call_target="Cholesky" | custom-call | tf_op jit(solution)/shard_map/jit(cholesky)/cholesky | solution.py:37
  326.9 4.4 while.7
  327.8 1.4 bitcast_dynamic-update-slice_fusion.5
  329.8 1.4 bitcast_dynamic-update-slice_fusion.5
  331.3 19.7 %custom-call.16 = f32[2,128,128]{1,2,0:T(8,128)S(1)} custom-call(f32[2,128,128]{2,1,0:T(8,128)S(1)} %get-tuple-element.46), custom_call_target="InvertDiagBlocksLowerTriangular" | custom-call | tf_op jit(solution)/shard_map/jit(_solve_triangular)/triangular_solve | solution.py:40
  353.6 37.8 %all-reduce.16.cloned.1.call-done = f32[2,256,256]{2,1,0:T(8,128)} async-done(((f32[2,256,256]{2,1,0:T(8,128)}), f32[2,256,256]{2,1,0:T(8,128)}) %all-reduce.16.cloned.1.call-update) | async-done | bytes 524304 | tf_op jit(solution)/shard_map/psum | solution.py:14
  391.4 2.2 broadcast_select_fusion
  394.6 1.0 copy.24
  395.6 1.3 select_dynamic-update-slice_fusion
  396.9 54.2 %all-reduce.18.cloned.1.call-done = f32[4,256,256]{2,1,0:T(8,128)} async-done(((f32[4,256,256]{2,1,0:T(8,128)}), f32[4,256,256]{2,1,0:T(8,128)}) %all-reduce.18.cloned.1.call-update) | async-done | bytes 1048592 | tf_op jit(solution)/shard_map/psum | solution.py:25
  451.0 4.5 select_bitcast_fusion
  455.5 6.0 %copy.27 = f32[2,1,256,4,1,256]{5,4,3,2,1,0:T(1,128)} copy(f32[2,1,256,4,1,256]{2,5,3,0,4,1:T(8,128)} %select_bitcast_fusion) | data formatting | bytes 4194304 | tf_op jit(solution)/shard_map/reshape | solution.py:84
  (77 shorter events, 18.2 us)
Async XLA Ops:
  6.5 61.7 %all-reduce.8.cloned.1.call-start = ((), (), s32[]{:S(2)}) async-start(), calls=%async_computation | async-start | bytes 524288 | tf_op jit(solution)/shard_map/psum | solution.py:14
  11.9 158.9 %all-reduce.10.cloned.1.call-start = ((), (), s32[]{:S(2)}) async-start(), calls=%async_computation.1 | async-start | bytes 1048576 | tf_op jit(solution)/shard_map/psum | solution.py:14
  132.9 97.9 %all-reduce.12.cloned.1.call-start = ((), (), s32[]{:S(2)}) async-start(), calls=%async_computation.2 | async-start | bytes 2097152 | tf_op jit(solution)/shard_map/psum | solution.py:25
  173.0 57.9 %copy-start.1 = (f32[2,256,256]{2,1,0:T(8,128)S(1)}, f32[2,256,256]{2,1,0:T(8,128)}, u32[]{:S(2)}) copy-start(f32[2,256,256]{2,1,0:T(8,128)} %all-reduce.10.cloned.1.call-done) | copy-start | bytes 1572868
  173.0 115.2 %all-reduce.14.cloned.1.call-start = ((), (), s32[]{:S(2)}) async-start(), calls=%async_computation.3 | async-start | bytes 524288 | tf_op jit(solution)/shard_map/psum | solution.py:14
  176.3 1.3 copy-start
  235.5 155.9 %all-reduce.16.cloned.1.call-start = ((), (), s32[]{:S(2)}) async-start(), calls=%async_computation.4 | async-start | bytes 1048576 | tf_op jit(solution)/shard_map/psum | solution.py:14
  353.6 97.4 %all-reduce.18.cloned.1.call-start = ((), (), s32[]{:S(2)}) async-start(), calls=%async_computation.5 | async-start | bytes 2097152 | tf_op jit(solution)/shard_map/psum | solution.py:25
  393.6 57.5 %copy-start.2 = (f32[2,256,256]{2,1,0:T(8,128)S(1)}, f32[2,256,256]{2,1,0:T(8,128)}, u32[]{:S(2)}) copy-start(f32[2,256,256]{2,1,0:T(8,128)} %all-reduce.16.cloned.1.call-done) | copy-start | bytes 1572868
Sparse Core Ops, SparseCore 0:
  12.0 56.1 all-reduce.7
  133.1 37.6 all-reduce.9
  174.3 56.5 all-reduce.11
  235.6 52.5 all-reduce.13
  353.7 37.6 all-reduce.15
  394.4 56.5 all-reduce.17
where the time goes:
time: 469 us; the launch traced here: 468 us
  waiting for transfers between devices  291 us (62%)
  other arithmetic  121 us (26%)
  local copies, waits for them, and re-layouts  26.9 us (6%)
  between operations  16.6 us (4%)
  matrix products  12.1 us (3%)
    psum x4, waiting for transfers between devices, from_root(): return lax.psum(jnp.where(mine, shard, jnp.zeros_like(shard)), axis)  184 us
    psum x2, waiting for transfers between devices, crossing_tiles(): gathered = lax.psum(buffer, 'row')  107 us
    another operation x13, other arithmetic, panel_step(): factor_diag = jnp.linalg.cholesky(corner)  68.7 us
    another operation x5, other arithmetic, panel_step(): jax.scipy.linalg.solve_triangular(factor_diag, flat.T, lower=True)  39.4 us
  transfers between devices with their start and end apart: 6, of which 6 were waited for; matrix products, arithmetic and copies ran while one was open for 1% of the time, Pallas kernels for 0%

commit v1 on v0

v1 whole, which is shorter than its diff:
```python
import functools

import jax
import jax.numpy as jnp
from jax import lax
from jax.experimental import pallas as pl
from jax.experimental.pallas import tpu as pltpu
from jax.sharding import PartitionSpec as P

NB = 256
HALF = 128
SUB = 8
HIGHEST = lax.Precision.HIGHEST
HIGH = lax.Precision.HIGH


def mm(a, b, precision=HIGHEST):
    return lax.dot_general(
        a, b, (((1,), (0,)), ((), ())), precision=precision, preferred_element_type=jnp.float32
    )


def mm_t(a, b, precision=HIGHEST):
    return lax.dot_general(
        a, b, (((1,), (1,)), ((), ())), precision=precision, preferred_element_type=jnp.float32
    )


def t_mm(a, b, precision=HIGHEST):
    return lax.dot_general(
        a, b, (((0,), (0,)), ((), ())), precision=precision, preferred_element_type=jnp.float32
    )


def spread(x):
    return jnp.broadcast_to(x, (SUB, HALF))


def factor_half(s):
    groups = HALF // SUB
    rows = [s[SUB * g : SUB * (g + 1), :] for g in range(groups)]
    lane = lax.broadcasted_iota(jnp.int32, (SUB, HALF), 1)
    sub = lax.broadcasted_iota(jnp.int32, (SUB, HALF), 0)
    eyes = [jnp.where(lane == sub + SUB * g, 1.0, 0.0).astype(jnp.float32) for g in range(groups)]
    out_u, out_x = [], []
    for g in range(groups):
        base = SUB * g
        own = rows[g]
        own_x = eyes[g]
        a = {}
        for i in range(SUB):
            for j in range(i, SUB):
                a[i, j] = spread(own[i : i + 1, base + j : base + j + 1])
        near = None
        if g + 1 < groups:
            near = [spread(rows[g + 1][:, base + j : base + j + 1]) for j in range(SUB)]
        u = [spread(own[i : i + 1, :]) for i in range(SUB)]
        x = [spread(own_x[i : i + 1, :]) for i in range(SUB)]
        r = [None] * SUB
        l = {}
        for k in range(SUB):
            r[k] = lax.rsqrt(a[k, k])
            for j in range(k + 1, SUB):
                l[k, j] = a[k, j] * r[k]
            for i in range(k + 1, SUB):
                for j in range(i, SUB):
                    a[i, j] = a[i, j] - l[k, i] * l[k, j]
            u[k] = u[k] * r[k]
            x[k] = x[k] * r[k]
            if near is not None:
                near[k] = near[k] * r[k]
            for i in range(k + 1, SUB):
                u[i] = u[i] - l[k, i] * u[k]
                x[i] = x[i] - l[k, i] * x[k]
                if near is not None:
                    near[i] = near[i] - l[k, i] * near[k]
        final_u, final_x = u[0], x[0]
        for i in range(1, SUB):
            final_u = jnp.where(sub == i, u[i], final_u)
            final_x = jnp.where(sub == i, x[i], final_x)
        out_u.append(jnp.where(lane >= sub + base, final_u, 0.0))
        out_x.append(final_x)
        if near is not None:
            nxt, nxt_x = rows[g + 1], eyes[g + 1]
            for k in range(SUB):
                nxt = nxt - near[k] * u[k]
                nxt_x = nxt_x - near[k] * x[k]
        if g + 2 < groups:
            v, vx = list(u), list(x)
            for i in reversed(range(SUB)):
                for j in range(i + 1, SUB):
                    v[i] = v[i] - l[i, j] * v[j]
                    vx[i] = vx[i] - l[i, j] * vx[j]
                v[i] = v[i] * r[i]
                vx[i] = vx[i] * r[i]
            for h in range(g + 2, groups):
                far, far_x = rows[h], eyes[h]
                for j in range(SUB):
                    c = spread(rows[h][:, base + j : base + j + 1])
                    far = far - c * v[j]
                    far_x = far_x - c * vx[j]
                rows[h], eyes[h] = far, far_x
        if near is not None:
            rows[g + 1], eyes[g + 1] = nxt, nxt_x
    return jnp.concatenate(out_u, axis=0), jnp.concatenate(out_x, axis=0)


def factor_tile(s, u_ref, x_ref):
    zero = jnp.zeros((HALF, HALF), jnp.float32)
    u11, x11 = factor_half(s[:HALF, :HALF])
    u12 = mm(x11, s[:HALF, HALF:])
    u22, x22 = factor_half(s[HALF:, HALF:] - t_mm(u12, u12))
    x21 = -mm(x22, t_mm(u12, x11))
    u_ref[:HALF, :HALF] = u11
    u_ref[:HALF, HALF:] = u12
    u_ref[HALF:, :HALF] = zero
    u_ref[HALF:, HALF:] = u22
    x_ref[:HALF, :HALF] = x11
    x_ref[:HALF, HALF:] = zero
    x_ref[HALF:, :HALF] = x21
    x_ref[HALF:, HALF:] = x22


def tile_from(ref, start, stride):
    return jnp.concatenate(
        [ref[pl.ds(start, NB, stride=stride), :], ref[pl.ds(start + 1, NB, stride=stride), :]], axis=1
    )


def first_kernel(a_ref, u_ref, x_ref):
    factor_tile(tile_from(a_ref, 0, 2), u_ref, x_ref)


def second_kernel(x0_ref, a01_ref, a11_ref, u_ref, x_ref, w_ref):
    x0 = x0_ref[...]
    u01 = mm(x0, tile_from(a01_ref, 0, 2))
    factor_tile(tile_from(a11_ref, 0, 2) - t_mm(u01, u01), u_ref, x_ref)
    w_ref[...] = -mm(x_ref[...], t_mm(u01, x0))


def last_kernel(loc_rows, loc_cols, pos, own, r0, r1, c0, c1, u0, x0, u1, x1, w, out):
    stride = 2 * loc_cols
    prows = []
    for a in range(loc_rows):
        b0, b1 = tile_from(r0, a * 2 * NB, 2), tile_from(r1, a * 2 * NB, 2)
        prows.append(
            (mm_t(b0, x0[...], HIGH), mm_t(b0, w[...], HIGH) + mm_t(b1, x1[...], HIGH))
        )
    for b in range(loc_cols):
        tile_col = pos[1] + b * pos[3]
        d0, d1 = tile_from(c0, 2 * b, stride), tile_from(c1, 2 * b, stride)
        q0 = mm(x0[...], d0, HIGH)
        q1 = mm(w[...], d0, HIGH) + mm(x1[...], d1, HIGH)
        for a in range(loc_rows):
            tile_row = pos[0] + a * pos[2]
            start = a * NB * stride + 2 * b

            def put(value, start=start):
                out[pl.ds(start, NB, stride=stride), :] = value[:, :HALF]
                out[pl.ds(start + 1, NB, stride=stride), :] = value[:, HALF:]

            @pl.when(tile_row < tile_col)
            def _():
                put(jnp.zeros((NB, NB), jnp.float32))

            @pl.when((tile_row >= tile_col) & (tile_col >= 2))
            def _():
                put(
                    tile_from(own, start, stride)
                    - (mm(prows[a][0], q0, HIGH) + mm(prows[a][1], q1, HIGH))
                )

            if b == 0:

                @pl.when((tile_row > 0) & (tile_col == 0))
                def _():
                    put(prows[a][0])

                @pl.when((tile_row > 1) & (tile_col == 1))
                def _():
                    put(prows[a][1])

                if a == 0:

                    @pl.when((tile_row == 0) & (tile_col == 0))
                    def _():
                        put(u0[...].T)

                    @pl.when((tile_row == 1) & (tile_col == 1))
                    def _():
                        put(u1[...].T)


VMEM = pl.BlockSpec(memory_space=pltpu.VMEM)
SMEM = pl.BlockSpec(memory_space=pltpu.SMEM)
TILE = jax.ShapeDtypeStruct((NB, NB), jnp.float32)


def call(kernel, out_shape, flops, *args, smem=0):
    return pl.pallas_call(
        kernel,
        out_shape=out_shape,
        in_specs=[SMEM] * smem + [VMEM] * (len(args) - smem),
        out_specs=jax.tree.map(lambda _: VMEM, out_shape),
        compiler_params=pltpu.CompilerParams(vmem_limit_bytes=48 * 2**20),
        cost_estimate=pl.CostEstimate(flops=flops, bytes_accessed=2**22, transcendentals=0),
    )(*args)


def on_device(n_row, n_col, trailing_in):
    row = lax.axis_index("row")
    col = lax.axis_index("col")
    loc_rows, _, _, loc_cols, _, _ = trailing_in.shape
    halves = 2 * loc_cols
    x = trailing_in.reshape(loc_rows, NB, halves, HALF)

    def send(value, pairs):
        flat = [(s[0] * n_col + s[1], d[0] * n_col + d[1]) for s, d in pairs]
        return lax.ppermute(value, ("row", "col"), flat)

    corner = x[0, :, :2, :]
    planes = range(n_col)
    evens = range(2, n_row, 2)

    a00 = jnp.where(
        col == 0, corner, sum(send(corner, [((0, 0), (0, z))]) for z in range(1, n_col))
    )
    a00 = jnp.where(row == 0, a00, sum(send(a00, [((0, z), (r, z)) for z in planes]) for r in evens))
    other = send(a00, [((r, z), (r + 1, z)) for z in planes for r in range(0, n_row, 2)])
    a00 = jnp.where(row % 2 == 0, a00, other)

    pair = jnp.where(
        col == 1,
        corner,
        sum(send(corner, [((i, 1), (i, z)) for i in (0, 1)]) for z in planes if z != 1),
    )
    pair = jnp.where(
        row < 2,
        pair,
        sum(send(pair, [((i, z), (r + i, z)) for z in planes for i in (0, 1)]) for r in evens),
    )
    swap = [((r, z), (r ^ 1, z)) for z in planes for r in range(n_row)]
    other = send(pair, swap)
    a01 = jnp.where(row % 2 == 0, pair, other)
    a11 = jnp.where(row % 2 == 0, other, pair)

    bits = [1 << k for k in range(1, (n_row - 1).bit_length())]
    top = x[0]
    holders = ([0], [1])
    for first, second in zip(bits, bits[::-1]):
        pairs = []
        for mine, bit in zip(holders, (first, second)):
            new = [(h, h ^ bit) for h in mine]
            mine.extend(d for _, d in new)
            pairs += new
        got = send(top, [((s, z), (d, z)) for z in planes for s, d in pairs])
        targets = jnp.array([d for _, d in pairs], jnp.int32)
        top = jnp.where(jnp.any(targets == row), got, top)
    other = send(top, swap)
    c0 = jnp.where(row % 2 == 0, top, other)
    c1 = jnp.where(row % 2 == 0, other, top)

    left = x[:, :, :2, :]
    rows = range(n_row)
    back = send(left, [((r, 1), (r, 0)) for r in rows])
    steps, here = [], left
    for k in range(n_col - 1):
        hops = [(k, k + 1)] + ([(k + 1, k + 2)] if k + 2 < n_col else [])
        here = send(here, [((r, s), (r, d)) for r in rows for s, d in hops])
        steps.append(here)
    r0 = jnp.where(col == 0, left, steps[0])
    for k in range(1, n_col - 1):
        r0 = jnp.where(col == k + 1, steps[k], r0)
    r1 = jnp.where(col == 0, back, left)
    for k in range(n_col - 2):
        r1 = jnp.where(col == k + 2, steps[k], r1)

    def flat(value):
        return value.reshape(-1, HALF)

    u0, x0 = call(first_kernel, [TILE] * 2, 2 * 10**9, flat(a00))
    u1, x1, w = call(second_kernel, [TILE] * 3, 2 * 10**9, x0, flat(a01), flat(a11))
    pos = jnp.stack([row, col, jnp.int32(n_row), jnp.int32(n_col)]).astype(jnp.int32)
    own = flat(x)
    out = call(
        functools.partial(last_kernel, loc_rows, loc_cols),
        jax.ShapeDtypeStruct(own.shape, jnp.float32),
        4 * 10**9,
        pos, own, flat(r0), flat(r1), flat(c0), flat(c1), u0, x0, u1, x1, w,
        smem=1,
    )
    return out.reshape(trailing_in.shape)


def solution(mesh):
    return jax.shard_map(
        functools.partial(on_device, mesh.shape["row"], mesh.shape["col"]),
        mesh=mesh,
        in_specs=(P(None, "row", None, None, "col", None),),
        out_specs=P(None, "row", None, None, "col", None),
        check_vma=False,
    )
```

time: 469 us -> 111 us (0.24)
  the two profiles are of different devices: /device:TPU:0 before, /device:TPU:20 now
where the time goes in v1:
time: 111 us
  waiting for transfers between devices  42.3 us (38%)
  Pallas kernels  28.7 us (26%)
  starting transfers between devices  23.6 us (21%)
  other arithmetic  10 us (9%)
  local copies, waits for them, and re-layouts  5.69 us (5%)
    ppermute x21, waiting for transfers between devices, send(): return lax.ppermute(value, ('row', 'col'), flat)  42.3 us
    pallas_call x3, Pallas kernels, call(): pl.pallas_call(kernel, out_shape=out_shape, in_specs=[SMEM] * smem + [VME...  28.7 us
    ppermute x21, starting transfers between devices, send(): return lax.ppermute(value, ('row', 'col'), flat)  23.6 us
    select_n x1, other arithmetic, on_device(): r1 = jnp.where(col == k + 2, steps[k], r1)  2.63 us
  transfers between devices with their start and end apart: 21, of which 3 were waited for; matrix products, arithmetic and copies ran while one was open for 12% of the time, Pallas kernels for 19%

profile of v1, /device:TPU:20, one launch (start us, length us, event | category | flops | bytes accessed | tf_op | source)
XLA Modules:
  0.0 110.7 jit_solution(17109600042144958471)
XLA Ops:
  0.0 2.0 %slice.11 = f32[1,1,256,4,1,256]{5,4,3,2,1,0:T(1,128)S(1)} slice(f32[2,1,256,4,1,256]{5,4,3,2,1,0:T(1,128)} %param.3), slice={[0:1], [0:1], [0:256], [0:4], [0:1], [0:256]} | slice | bytes 2097152 | tf_op jit(solution)/shard_map/slice | solution.py:248
  2.0 0.7 collective-permute-start.4
  2.7 2.0 %slice_bitcast_fusion = f32[256,2,128]{2,1,0:T(2,128)} fusion(f32[2,256,8,128]{3,2,1,0:T(8,128)} %bitcast.45), kind=kLoop, calls=%fused_computation.6 | loop fusion | bytes 524288 | tf_op jit(solution)/shard_map/squeeze | solution.py:221
  5.4 1.4 %collective-permute-start.14 = (f32[256,2,128]{2,1,0:T(2,128)}, f32[256,2,128]{2,1,0:T(2,128)}, u32[]{:S(2)}, u32[]{:S(2)}) collective-permute-start(f32[256,2,128]{2,1,0:T(2,128)} %slice_bitcast_fusion), channel_id=1, source_target_pairs={{1,0},{5,4}} | collective-permute-start | bytes 786440 | tf_op jit(solution)/shard_map/ppermute | solution.py:219
  6.7 1.4 %collective-permute-start.15 = (f32[256,2,128]{2,1,0:T(2,128)}, f32[256,2,128]{2,1,0:T(2,128)}, u32[]{:S(2)}, u32[]{:S(2)}) collective-permute-start(f32[256,2,128]{2,1,0:T(2,128)} %slice_bitcast_fusion), channel_id=1, source_target_pairs={{1,2},{5,6}} | collective-permute-start | bytes 786440 | tf_op jit(solution)/shard_map/ppermute | solution.py:219
  8.1 1.4 %collective-permute-start.9 = (f32[256,2,128]{2,1,0:T(2,128)}, f32[256,2,128]{2,1,0:T(2,128)}, u32[]{:S(2)}, u32[]{:S(2)}) collective-permute-start(f32[256,2,128]{2,1,0:T(2,128)} %slice_bitcast_fusion), channel_id=1, source_target_pairs={{0,3}} | collective-permute-start | bytes 786440 | tf_op jit(solution)/shard_map/ppermute | solution.py:219
  9.4 0.7 compare_reduce_fusion
  10.8 0.7 collective-permute-start.8
  11.5 0.7 broadcast_select_fusion
  12.3 1.3 %collective-permute-start.5 = (f32[256,8,128]{2,1,0:T(8,128)S(1)}, f32[256,8,128]{2,1,0:T(8,128)S(1)}, u32[]{:S(2)}, u32[]{:S(2)}) collective-permute-start(f32[256,8,128]{2,1,0:T(8,128)S(1)} %broadcast_select_fusion), channel_id=1, source_target_pairs={{0,16},{8,24},{4,12},{20,28},{1,17},{9,25},{5,13},{21,29},{2,18},{... | collective-permute-start | bytes 3145736 | tf_op jit(solution)/shard_map/ppermute | solution.py:219
  13.6 2.0 %add_select_fusion.1 = (f32[256,2,128]{2,1,0:T(2,128)S(1)}, f32[256,2,128]{2,1,0:T(2,128)S(1)}) fusion(f32[256,2,128]{2,1,0:T(2,128)S(1)} %collective-permute-done.16, f32[256,2,128]{2,1,0:T(2,128)} %collective-permute-done.14, f32[256,2,128]{2,1,0:T(2,128)} %collective-permute-done.15, pred[]{:T(512)S(6)} %eq.53, f32[2,256,8,128]{3,2,1,0:T(8,128)} %bitcast.46, ...), kind=kLoop, calls=%fused_computation.8 | loop fusion | flops 393216 | bytes 2359298 | tf_op jit(solution)/shard_map/jit(_where)/select_n | solution.py:232
  16.3 1.4 %collective-permute-start.10 = (f32[256,2,128]{2,1,0:T(2,128)S(1)}, f32[256,2,128]{2,1,0:T(2,128)}, u32[]{:S(2)}, u32[]{:S(2)}) collective-permute-start(f32[256,2,128]{2,1,0:T(2,128)S(1)} %get-tuple-element.18), channel_id=1, source_target_pairs={{0,8},{1,9},{2,10},{3,11}} | collective-permute-start | bytes 786440 | tf_op jit(solution)/shard_map/ppermute | solution.py:219
  17.7 1.3 %collective-permute-start.11 = (f32[256,2,128]{2,1,0:T(2,128)S(1)}, f32[256,2,128]{2,1,0:T(2,128)}, u32[]{:S(2)}, u32[]{:S(2)}) collective-permute-start(f32[256,2,128]{2,1,0:T(2,128)S(1)} %get-tuple-element.18), channel_id=1, source_target_pairs={{0,16},{1,17},{2,18},{3,19}} | collective-permute-start | bytes 786440 | tf_op jit(solution)/shard_map/ppermute | solution.py:219
  18.9 1.7 %slice.13 = f32[2,256,2,128]{3,2,1,0:T(2,128)S(1)} slice(f32[2,256,8,128]{3,2,1,0:T(8,128)} %bitcast.47), slice={[0:2], [0:256], [0:2], [0:128]} | slice | bytes 1048576 | tf_op jit(solution)/shard_map/slice | solution.py:263
  20.7 1.3 %collective-permute-start = (f32[2,256,2,128]{3,2,1,0:T(2,128)S(1)}, f32[2,256,2,128]{3,2,1,0:T(2,128)}, u32[]{:S(2)}, u32[]{:S(2)}) collective-permute-start(f32[2,256,2,128]{3,2,1,0:T(2,128)S(1)} %slice.13), channel_id=1, source_target_pairs={{0,1},{1,2},{4,5},{5,6},{8,9},{9,10},{12,13},{13,14},{16,17},{17,1... | collective-permute-start | bytes 1572872 | tf_op jit(solution)/shard_map/ppermute | solution.py:219
  22.6 1.4 %collective-permute-start.19 = (f32[256,2,128]{2,1,0:T(2,128)S(1)}, f32[256,2,128]{2,1,0:T(2,128)}, u32[]{:S(2)}, u32[]{:S(2)}) collective-permute-start(f32[256,2,128]{2,1,0:T(2,128)S(1)} %get-tuple-element.17), channel_id=1, source_target_pairs={{0,24},{4,28},{1,25},{5,29},{2,26},{6,30},{3,27},{7,31}} | collective-permute-start | bytes 786440 | tf_op jit(solution)/shard_map/ppermute | solution.py:219
  24.0 1.3 %collective-permute-start.17 = (f32[256,2,128]{2,1,0:T(2,128)S(1)}, f32[256,2,128]{2,1,0:T(2,128)}, u32[]{:S(2)}, u32[]{:S(2)}) collective-permute-start(f32[256,2,128]{2,1,0:T(2,128)S(1)} %get-tuple-element.17), channel_id=1, source_target_pairs={{0,8},{4,12},{1,9},{5,13},{2,10},{6,14},{3,11},{7,15}} | collective-permute-start | bytes 786440 | tf_op jit(solution)/shard_map/ppermute | solution.py:219
  25.3 21.6 %collective-permute-done.11 = f32[256,2,128]{2,1,0:T(2,128)} collective-permute-done((f32[256,2,128]{2,1,0:T(2,128)S(1)}, f32[256,2,128]{2,1,0:T(2,128)}, u32[]{:S(2)}, u32[]{:S(2)}) %collective-permute-start.11) | collective-permute-done | bytes 262176 | tf_op jit(solution)/shard_map/ppermute | solution.py:219
  46.9 1.3 %collective-permute-start.18 = (f32[256,2,128]{2,1,0:T(2,128)S(1)}, f32[256,2,128]{2,1,0:T(2,128)}, u32[]{:S(2)}, u32[]{:S(2)}) collective-permute-start(f32[256,2,128]{2,1,0:T(2,128)S(1)} %get-tuple-element.17), channel_id=1, source_target_pairs={{0,16},{4,20},{1,17},{5,21},{2,18},{6,22},{3,19},{7,23}} | collective-permute-start | bytes 786440 | tf_op jit(solution)/shard_map/ppermute | solution.py:219
  48.3 1.1 %add_select_fusion.2 = f32[64,8,128]{2,1,0:T(8,128)S(1)} fusion(f32[64,8,128]{2,1,0:T(8,128)S(1)} %bitcast.51, f32[64,8,128]{2,1,0:T(8,128)S(1)} %bitcast.54, f32[64,8,128]{2,1,0:T(8,128)} %bitcast.23, f32[64,8,128]{2,1,0:T(8,128)} %bitcast.24, pred[]{:T(512)S(6)} %eq.52), kind=kLoop, calls=%fused_computation.9 | loop fusion | flops 196608 | bytes 1310721 | tf_op jit(solution)/shard_map/jit(_where)/select_n | solution.py:228
  49.4 0.7 collective-permute-start.3
  50.2 1.3 %collective-permute-start.13 = (f32[256,2,128]{2,1,0:T(2,128)S(1)}, f32[256,2,128]{2,1,0:T(2,128)S(1)}, u32[]{:S(2)}, u32[]{:S(2)}) collective-permute-start(f32[256,2,128]{2,1,0:T(2,128)S(1)} %bitcast.52), channel_id=1, source_target_pairs={{0,4},{8,12},{16,20},{24,28},{1,5},{9,13},{17,21},{25,29},{2,6},{1... | collective-permute-start | bytes 786440 | tf_op jit(solution)/shard_map/ppermute | solution.py:219
  51.5 7.5 %collective-permute-done.18 = f32[256,2,128]{2,1,0:T(2,128)} collective-permute-done((f32[256,2,128]{2,1,0:T(2,128)S(1)}, f32[256,2,128]{2,1,0:T(2,128)}, u32[]{:S(2)}, u32[]{:S(2)}) %collective-permute-start.18) | collective-permute-done | bytes 262176 | tf_op jit(solution)/shard_map/ppermute | solution.py:219
  58.9 1.2 %add_select_fusion = f32[64,8,128]{2,1,0:T(8,128)S(1)} fusion(f32[64,8,128]{2,1,0:T(8,128)S(1)} %bitcast.50, f32[64,8,128]{2,1,0:T(8,128)} %bitcast.30, f32[64,8,128]{2,1,0:T(8,128)} %bitcast.31, f32[64,8,128]{2,1,0:T(8,128)} %bitcast.32, pred[]{:T(512)S(6)} %lt.18), kind=kLoop, calls=%fused_computation.7 | loop fusion | flops 196608 | bytes 1310721 | tf_op jit(solution)/shard_map/jit(_where)/select_n | solution.py:237
  60.2 1.9 %collective-permute-start.1 = (f32[2,256,2,128]{3,2,1,0:T(2,128)}, f32[2,256,2,128]{3,2,1,0:T(2,128)S(1)}, u32[]{:S(2)}, u32[]{:S(2)}) collective-permute-start(f32[2,256,2,128]{3,2,1,0:T(2,128)} %collective-permute-done), channel_id=1, source_target_pairs={{1,2},{2,3},{5,6},{6,7},{9,10},{10,11},{13,14},{14,15},{17,18},{18... | collective-permute-start | bytes 1572872 | tf_op jit(solution)/shard_map/ppermute | solution.py:219
  62.2 0.8 broadcast_select_fusion.1
  63.5 13.1 %collective-permute-done.1 = f32[2,256,2,128]{3,2,1,0:T(2,128)S(1)} collective-permute-done((f32[2,256,2,128]{3,2,1,0:T(2,128)}, f32[2,256,2,128]{3,2,1,0:T(2,128)S(1)}, u32[]{:S(2)}, u32[]{:S(2)}) %collective-permute-start.1) | collective-permute-done | bytes 524320 | tf_op jit(solution)/shard_map/ppermute | solution.py:219
  76.6 2.4 %collective-permute-start.2 = (f32[2,256,2,128]{3,2,1,0:T(2,128)S(1)}, f32[2,256,2,128]{3,2,1,0:T(2,128)S(1)}, u32[]{:S(2)}, u32[]{:S(2)}) collective-permute-start(f32[2,256,2,128]{3,2,1,0:T(2,128)S(1)} %collective-permute-done.1), channel_id=1, source_target_pairs={{2,3},{6,7},{10,11},{14,15},{18,19},{22,23},{26,27},{30,31}} | collective-permute-start | bytes 1572872 | tf_op jit(solution)/shard_map/ppermute | solution.py:219
  79.0 9.7 %shard_map.37 = (f32[256,256]{1,0:T(8,128)S(1)}, f32[256,256]{1,0:T(8,128)S(1)}) custom-call(f32[512,128]{1,0:T(8,128)S(1)} %bitcast.40), custom_call_target="tpu_custom_call" | custom-call | flops 2000000000 | bytes 4194304 | tf_op jit(solution)/shard_map/pallas_call | solution.py:200
  88.8 11.3 %shard_map.38 = (f32[256,256]{1,0:T(8,128)S(1)}, f32[256,256]{1,0:T(8,128)S(1)}, f32[256,256]{1,0:T(8,128)S(1)}) custom-call(f32[256,256]{1,0:T(8,128)S(1)} %get-tuple-element.11.x0_ref.x0, f32[512,128]{1,0:T(8,128)S(1)} %bitcast.42, f32[512,128]{1,0:T(8,128)S(1)} %bitcast.41), custom_call_target="tpu_custom_call" | custom-call | flops 2000000000 | bytes 4194304 | tf_op jit(solution)/shard_map/pallas_call | solution.py:200
  100.1 2.6 %select_select_fusion = (f32[2,256,2,128]{3,2,1,0:T(2,128)S(1)}, f32[2,256,2,128]{3,2,1,0:T(2,128)S(1)}) fusion(f32[2,256,2,128]{3,2,1,0:T(2,128)S(1)} %collective-permute-done.1, f32[2,256,2,128]{3,2,1,0:T(2,128)} %collective-permute-done, f32[2,256,2,128]{3,2,1,0:T(2,128)S(1)} %collective-permute-done.3, pred[]{:T(512)S(6)} %eq.46, pred[]{:T(512)S(6)} %eq.45, ...), kind=kLoop, calls=%fused_computation.2 | loop fusion | flops 786432 | bytes 3670019 | tf_op jit(solution)/shard_map/jit(_where)/select_n | solution.py:276
  102.9 7.7 %shard_map.39 = f32[4096,128]{1,0:T(8,128)} custom-call(s32[4]{0:T(128)S(1)} %pad_add_fusion.pos, f32[4096,128]{1,0:T(8,128)} %bitcast.49, f32[1024,128]{1,0:T(8,128)S(1)} %bitcast.39, f32[1024,128]{1,0:T(8,128)S(1)} %bitcast.38, f32[2048,128]{1,0:T(8,128)S(1)} %get-tuple-element.20.c0, f32[2048,128]{1,0:T(8,128)S(1)} %get-tuple-element.19.c1, ...), custom_call_target="tpu_custom_call" | custom-call | flops 4000000000 | bytes 4194304 | tf_op jit(solution)/shard_map/pallas_call | solution.py:200
  (32 shorter events, 3.6 us)
Async XLA Ops:
  0.0 9.4 %copy-start.1 = (s32[2]{0:T(128)S(1)}, s32[2]{0:T(128)}, u32[]{:S(2)}) copy-start(s32[2]{0:T(128)} %constant.44.clone) | copy-start | bytes 28
  2.0 8.9 %collective-permute-start.4 = (f32[256,8,128]{2,1,0:T(8,128)S(1)}, f32[256,8,128]{2,1,0:T(8,128)S(1)}, u32[]{:S(2)}, u32[]{:S(2)}) collective-permute-start(f32[256,8,128]{2,1,0:T(8,128)S(1)} %bitcast.43), channel_id=1, source_target_pairs={{0,8},{4,20},{1,9},{5,21},{2,10},{6,22},{3,11},{7,23}} | collective-permute-start | bytes 3145736 | tf_op jit(solution)/shard_map/ppermute | solution.py:219
  4.7 5.4 %collective-permute-start.16 = (f32[256,2,128]{2,1,0:T(2,128)}, f32[256,2,128]{2,1,0:T(2,128)S(1)}, u32[]{:S(2)}, u32[]{:S(2)}) collective-permute-start(f32[256,2,128]{2,1,0:T(2,128)} %slice_bitcast_fusion), channel_id=1, source_target_pairs={{1,3},{5,7}} | collective-permute-start | bytes 786440 | tf_op jit(solution)/shard_map/ppermute | solution.py:219
  5.4 6.9 %collective-permute-start.14 = (f32[256,2,128]{2,1,0:T(2,128)}, f32[256,2,128]{2,1,0:T(2,128)}, u32[]{:S(2)}, u32[]{:S(2)}) collective-permute-start(f32[256,2,128]{2,1,0:T(2,128)} %slice_bitcast_fusion), channel_id=1, source_target_pairs={{1,0},{5,4}} | collective-permute-start | bytes 786440 | tf_op jit(solution)/shard_map/ppermute | solution.py:219
  6.7 6.8 %collective-permute-start.15 = (f32[256,2,128]{2,1,0:T(2,128)}, f32[256,2,128]{2,1,0:T(2,128)}, u32[]{:S(2)}, u32[]{:S(2)}) collective-permute-start(f32[256,2,128]{2,1,0:T(2,128)} %slice_bitcast_fusion), channel_id=1, source_target_pairs={{1,2},{5,6}} | collective-permute-start | bytes 786440 | tf_op jit(solution)/shard_map/ppermute | solution.py:219
  8.1 5.5 %collective-permute-start.9 = (f32[256,2,128]{2,1,0:T(2,128)}, f32[256,2,128]{2,1,0:T(2,128)}, u32[]{:S(2)}, u32[]{:S(2)}) collective-permute-start(f32[256,2,128]{2,1,0:T(2,128)} %slice_bitcast_fusion), channel_id=1, source_target_pairs={{0,3}} | collective-permute-start | bytes 786440 | tf_op jit(solution)/shard_map/ppermute | solution.py:219
  10.1 3.5 %collective-permute-start.7 = (f32[256,2,128]{2,1,0:T(2,128)}, f32[256,2,128]{2,1,0:T(2,128)S(1)}, u32[]{:S(2)}, u32[]{:S(2)}) collective-permute-start(f32[256,2,128]{2,1,0:T(2,128)} %slice_bitcast_fusion), channel_id=1, source_target_pairs={{0,1}} | collective-permute-start | bytes 786440 | tf_op jit(solution)/shard_map/ppermute | solution.py:219
  10.8 2.8 %collective-permute-start.8 = (f32[256,2,128]{2,1,0:T(2,128)}, f32[256,2,128]{2,1,0:T(2,128)S(1)}, u32[]{:S(2)}, u32[]{:S(2)}) collective-permute-start(f32[256,2,128]{2,1,0:T(2,128)} %slice_bitcast_fusion), channel_id=1, source_target_pairs={{0,2}} | collective-permute-start | bytes 786440 | tf_op jit(solution)/shard_map/ppermute | solution.py:219
  12.2 9.7 %copy-start = (s32[4]{0:T(128)S(1)}, s32[4]{0:T(128)}, u32[]{:S(2)}) copy-start(s32[4]{0:T(128)} %constant.45.clone) | copy-start | bytes 52
  12.3 49.9 %collective-permute-start.5 = (f32[256,8,128]{2,1,0:T(8,128)S(1)}, f32[256,8,128]{2,1,0:T(8,128)S(1)}, u32[]{:S(2)}, u32[]{:S(2)}) collective-permute-start(f32[256,8,128]{2,1,0:T(8,128)S(1)} %broadcast_select_fusion), channel_id=1, source_target_pairs={{0,16},{8,24},{4,12},{20,28},{1,17},{9,25},{5,13},{21,29},{2,18},{... | collective-permute-start | bytes 3145736 | tf_op jit(solution)/shard_map/ppermute | solution.py:219
  15.6 7.0 %collective-permute-start.12 = (f32[256,2,128]{2,1,0:T(2,128)S(1)}, f32[256,2,128]{2,1,0:T(2,128)S(1)}, u32[]{:S(2)}, u32[]{:S(2)}) collective-permute-start(f32[256,2,128]{2,1,0:T(2,128)S(1)} %get-tuple-element.18), channel_id=1, source_target_pairs={{0,24},{1,25},{2,26},{3,27}} | collective-permute-start | bytes 786440 | tf_op jit(solution)/shard_map/ppermute | solution.py:219
  16.3 7.7 %collective-permute-start.10 = (f32[256,2,128]{2,1,0:T(2,128)S(1)}, f32[256,2,128]{2,1,0:T(2,128)}, u32[]{:S(2)}, u32[]{:S(2)}) collective-permute-start(f32[256,2,128]{2,1,0:T(2,128)S(1)} %get-tuple-element.18), channel_id=1, source_target_pairs={{0,8},{1,9},{2,10},{3,11}} | collective-permute-start | bytes 786440 | tf_op jit(solution)/shard_map/ppermute | solution.py:219
  17.7 29.3 %collective-permute-start.11 = (f32[256,2,128]{2,1,0:T(2,128)S(1)}, f32[256,2,128]{2,1,0:T(2,128)}, u32[]{:S(2)}, u32[]{:S(2)}) collective-permute-start(f32[256,2,128]{2,1,0:T(2,128)S(1)} %get-tuple-element.18), channel_id=1, source_target_pairs={{0,16},{1,17},{2,18},{3,19}} | collective-permute-start | bytes 786440 | tf_op jit(solution)/shard_map/ppermute | solution.py:219
  20.7 39.5 %collective-permute-start = (f32[2,256,2,128]{3,2,1,0:T(2,128)S(1)}, f32[2,256,2,128]{3,2,1,0:T(2,128)}, u32[]{:S(2)}, u32[]{:S(2)}) collective-permute-start(f32[2,256,2,128]{3,2,1,0:T(2,128)S(1)} %slice.13), channel_id=1, source_target_pairs={{0,1},{1,2},{4,5},{5,6},{8,9},{9,10},{12,13},{13,14},{16,17},{17,1... | collective-permute-start | bytes 1572872 | tf_op jit(solution)/shard_map/ppermute | solution.py:219
  22.6 26.8 %collective-permute-start.19 = (f32[256,2,128]{2,1,0:T(2,128)S(1)}, f32[256,2,128]{2,1,0:T(2,128)}, u32[]{:S(2)}, u32[]{:S(2)}) collective-permute-start(f32[256,2,128]{2,1,0:T(2,128)S(1)} %get-tuple-element.17), channel_id=1, source_target_pairs={{0,24},{4,28},{1,25},{5,29},{2,26},{6,30},{3,27},{7,31}} | collective-permute-start | bytes 786440 | tf_op jit(solution)/shard_map/ppermute | solution.py:219
  24.0 26.2 %collective-permute-start.17 = (f32[256,2,128]{2,1,0:T(2,128)S(1)}, f32[256,2,128]{2,1,0:T(2,128)}, u32[]{:S(2)}, u32[]{:S(2)}) collective-permute-start(f32[256,2,128]{2,1,0:T(2,128)S(1)} %get-tuple-element.17), channel_id=1, source_target_pairs={{0,8},{4,12},{1,9},{5,13},{2,10},{6,14},{3,11},{7,15}} | collective-permute-start | bytes 786440 | tf_op jit(solution)/shard_map/ppermute | solution.py:219
  46.9 12.0 %collective-permute-start.18 = (f32[256,2,128]{2,1,0:T(2,128)S(1)}, f32[256,2,128]{2,1,0:T(2,128)}, u32[]{:S(2)}, u32[]{:S(2)}) collective-permute-start(f32[256,2,128]{2,1,0:T(2,128)S(1)} %get-tuple-element.17), channel_id=1, source_target_pairs={{0,16},{4,20},{1,17},{5,21},{2,18},{6,22},{3,19},{7,23}} | collective-permute-start | bytes 786440 | tf_op jit(solution)/shard_map/ppermute | solution.py:219
  49.4 50.7 %collective-permute-start.3 = (f32[2,256,2,128]{3,2,1,0:T(2,128)S(1)}, f32[2,256,2,128]{3,2,1,0:T(2,128)S(1)}, u32[]{:S(2)}, u32[]{:S(2)}) collective-permute-start(f32[2,256,2,128]{3,2,1,0:T(2,128)S(1)} %slice.13), channel_id=1, source_target_pairs={{1,0},{5,4},{9,8},{13,12},{17,16},{21,20},{25,24},{29,28}} | collective-permute-start | bytes 1572872 | tf_op jit(solution)/shard_map/ppermute | solution.py:219
  50.2 13.3 %collective-permute-start.13 = (f32[256,2,128]{2,1,0:T(2,128)S(1)}, f32[256,2,128]{2,1,0:T(2,128)S(1)}, u32[]{:S(2)}, u32[]{:S(2)}) collective-permute-start(f32[256,2,128]{2,1,0:T(2,128)S(1)} %bitcast.52), channel_id=1, source_target_pairs={{0,4},{8,12},{16,20},{24,28},{1,5},{9,13},{17,21},{25,29},{2,6},{1... | collective-permute-start | bytes 786440 | tf_op jit(solution)/shard_map/ppermute | solution.py:219
  60.1 28.6 %collective-permute-start.20 = (f32[256,2,128]{2,1,0:T(2,128)S(1)}, f32[256,2,128]{2,1,0:T(2,128)S(1)}, u32[]{:S(2)}, u32[]{:S(2)}) collective-permute-start(f32[256,2,128]{2,1,0:T(2,128)S(1)} %bitcast.53), channel_id=1, source_target_pairs={{0,4},{4,0},{8,12},{12,8},{16,20},{20,16},{24,28},{28,24},{1,5},{5... | collective-permute-start | bytes 786440 | tf_op jit(solution)/shard_map/ppermute | solution.py:219
  60.2 16.4 %collective-permute-start.1 = (f32[2,256,2,128]{3,2,1,0:T(2,128)}, f32[2,256,2,128]{3,2,1,0:T(2,128)S(1)}, u32[]{:S(2)}, u32[]{:S(2)}) collective-permute-start(f32[2,256,2,128]{3,2,1,0:T(2,128)} %collective-permute-done), channel_id=1, source_target_pairs={{1,2},{2,3},{5,6},{6,7},{9,10},{10,11},{13,14},{14,15},{17,18},{18... | collective-permute-start | bytes 1572872 | tf_op jit(solution)/shard_map/ppermute | solution.py:219
  62.9 39.8 %collective-permute-start.6 = (f32[256,8,128]{2,1,0:T(8,128)S(1)}, f32[256,8,128]{2,1,0:T(8,128)S(1)}, u32[]{:S(2)}, u32[]{:S(2)}) collective-permute-start(f32[256,8,128]{2,1,0:T(8,128)S(1)} %broadcast_select_fusion.1), channel_id=1, source_target_pairs={{0,4},{4,0},{8,12},{12,8},{16,20},{20,16},{24,28},{28,24},{1,5},{5... | collective-permute-start | bytes 3145736 | tf_op jit(solution)/shard_map/ppermute | solution.py:219
  76.6 23.5 %collective-permute-start.2 = (f32[2,256,2,128]{3,2,1,0:T(2,128)S(1)}, f32[2,256,2,128]{3,2,1,0:T(2,128)S(1)}, u32[]{:S(2)}, u32[]{:S(2)}) collective-permute-start(f32[2,256,2,128]{3,2,1,0:T(2,128)S(1)} %collective-permute-done.1), channel_id=1, source_target_pairs={{2,3},{6,7},{10,11},{14,15},{18,19},{22,23},{26,27},{30,31}} | collective-permute-start | bytes 1572872 | tf_op jit(solution)/shard_map/ppermute | solution.py:219
